TPU v7x, 32 devices: a whole 2x2x4 slice. The times are simulated.
32 devices in a mesh: grp: 2 (over y), mom: 16 (over z, x, core).
Axes of the slice: x: 2, y: 2, z: 4, core: 2. Of those that a mesh axis runs over, the one named last changes fastest.
Arguments:
- green_function: bfloat16 [2, 4096, 512], P(None, ('grp', 'mom')), parts along dimension 1, may hold values from -0.8984375 to 0.8984375
- couplings: bfloat16 [8, 2, 512, 512], replicated, may hold values from -0.1875 to 0.1875
- phonon_modes: int32 [3, 4], replicated, may hold values from 0 to 7
- weights: float32 [3, 4], replicated, may hold values from 0.5 to 2
Outputs:
- self_energy: float32 [2, 4096, 512], P(None, ('grp', 'mom')), parts along dimension 1
There are 2 independent parts, one for each index of `grp`. A program takes and returns all parts, laid end to end along the dimension named above; an argument that names none is the same for every part. Nothing has to cross between parts.
Inputs may be any that keep to these rules, and one draw needn't show every extreme that they name: `phonon_modes`: each entry names one matrix of couplings.
All inputs are finite; a program needn't handle non-finite values.
Results may differ from a plain program's by a relative error of at most 0.0042.
Values may be sent and summed in bfloat16 or wider, within the bound.
A program may use at most 64 MiB of HBM per device.

v0:
```python
import jax
import jax.numpy as jnp
import numpy as np
from jax import lax
from jax.sharding import PartitionSpec as P


def partner(block, axis, bit):
    count = lax.axis_size(axis)
    route = []
    for low in range(count):
        high = low | 1 << bit
        if high != low and high < count:
            route += [(low, high), (high, low)]
    return lax.ppermute(block, axis, route)


def passed_along(block, axis, distance):
    devices = range(lax.axis_size(axis))
    route = [((i - distance) % len(devices), i) for i in devices]
    return lax.ppermute(block, axis, route)


def stack_spectral(spectral):
    upper_half = jnp.concatenate([spectral[0], spectral[1]], axis=1)
    lower_half = jnp.concatenate([-spectral[1], spectral[0]], axis=1)
    return jnp.concatenate([upper_half, lower_half], axis=0)


def stack_coupling(coupling):
    upper_half = jnp.concatenate([coupling[0], coupling[1]], axis=1)
    lower_half = jnp.concatenate([-coupling[1], coupling[0]], axis=1)
    return jnp.concatenate([upper_half, lower_half], axis=0)


def place_pair(gathered, received, member, level):
    upper_half = member >> level & 1
    return jnp.where(
        upper_half == 1,
        jnp.concatenate([received, gathered]),
        jnp.concatenate([gathered, received]),
    )


def collect_own_rows(local_piece, levels, member):
    gathered = local_piece[None]
    for level in range(levels):
        received = partner(gathered, "mom", level)
        gathered = place_pair(gathered, received, member, level)
    return gathered


def as_slab(row_blocks):
    group_size, parts, tile_rows, slab_order = row_blocks.shape
    return row_blocks.transpose(1, 0, 2, 3).reshape(parts, group_size * tile_rows, slab_order)


def stop_term(spectral, stop_index, couplings, phonon_modes, weights, member, tile_rows):
    stacked = stack_spectral(spectral)
    mode_count = phonon_modes.shape[1]
    left_list = []
    right_list = []
    for mode_index in range(mode_count):
        coupling = lax.dynamic_index_in_dim(
            couplings, phonon_modes[stop_index, mode_index], 0, keepdims=False
        )
        coupled_rows = lax.dynamic_slice_in_dim(coupling, member * tile_rows, tile_rows, 1)
        left_list.append(jnp.concatenate([coupled_rows[0], coupled_rows[1]], axis=1))
        right_list.append(stack_coupling(coupling))
    products = jnp.dot(
        jnp.concatenate(left_list, axis=0), stacked, preferred_element_type=jnp.float32
    ).astype(jnp.bfloat16)
    total = None
    for mode_index in range(mode_count):
        product = products[mode_index * tile_rows : (mode_index + 1) * tile_rows]
        contribution = lax.dot_general(
            product,
            right_list[mode_index],
            (((1,), (1,)), ((), ())),
            preferred_element_type=jnp.float32,
        )
        weighted = weights[stop_index, mode_index] * contribution
        total = weighted if total is None else total + weighted
    return total


def body(green_function, couplings, phonon_modes, weights):
    tile_rows = green_function.shape[1]
    slab_order = green_function.shape[2]
    group_size = slab_order // tile_rows
    levels = group_size.bit_length() - 1
    member = lax.axis_index("mom") % group_size
    stop_count = phonon_modes.shape[0]
    reach = (stop_count - 1) // 2
    whole_spectral = None
    blocks = green_function.reshape(2, tile_rows, group_size, tile_rows).transpose(2, 0, 1, 3)
    partner_order = jnp.arange(group_size, dtype=jnp.int32) ^ member
    mirror_slots = jnp.take(blocks, partner_order, axis=0)
    for level in range(levels):
        chosen = [slot_index for slot_index in range(group_size) if slot_index >> level & 1]
        picked = jnp.stack([mirror_slots[slot_index] for slot_index in chosen])
        arrived = partner(picked, "mom", level)
        mirror_slots = mirror_slots.at[np.array(chosen)].set(arrived)
    mirrored = jnp.take(mirror_slots, partner_order, axis=0)
    mirror_rows = jnp.transpose(mirrored, (1, 3, 0, 2)).reshape(2, tile_rows, slab_order)
    spec_real = -(green_function[1].astype(jnp.float32) + mirror_rows[1].astype(jnp.float32))
    spec_imag = green_function[0].astype(jnp.float32) - mirror_rows[0].astype(jnp.float32)
    own_rows = jnp.stack([spec_real, spec_imag]).astype(jnp.bfloat16)
    whole_spectral = as_slab(collect_own_rows(own_rows, levels, member))
    terms = [
        stop_term(whole_spectral, stop_index, couplings, phonon_modes, weights, member, tile_rows)
        for stop_index in range(stop_count)
    ]
    accumulated = terms[reach]
    carried = terms[stop_count - 1]
    carried = passed_along(carried, "mom", group_size)
    accumulated = accumulated + carried
    carried = terms[0]
    carried = passed_along(carried, "mom", -group_size)
    accumulated = accumulated + carried
    return accumulated.reshape(tile_rows, 2, slab_order).transpose(1, 0, 2)


def solution(mesh):
    in_specs = (P(None, ("grp", "mom"), None), P(), P(), P())
    out_specs = P(None, ("grp", "mom"), None)
    return jax.shard_map(body, mesh=mesh, in_specs=in_specs, out_specs=out_specs, check_vma=False)
```

profile of v0, /device:TPU:0, one launch (start us, length us, event | category | flops | bytes accessed | tf_op | source)
XLA Modules:
  0.0 94.2 jit_solution(5716834924307445345)
XLA Ops:
  0.0 1.1 %copy.13 = bf16[2,128,512]{1,2,0:T(8,128)(2,1)S(1)} copy(bf16[2,128,512]{2,1,0:T(8,128)(2,1)} %param.10) | data formatting | bytes 524288 | tf_op args[0]
  1.2 0.2 copy.14
  1.4 0.6 gather_fusion
  2.0 0.1 broadcast_select_fusion
  2.1 0.5 collective-permute-start
  2.6 0.7 fusion.256
  25.9 0.6 scatter_fusion
  26.6 2.6 %collective-permute-start.1 = (bf16[2,2,128,128]{3,2,1,0:T(8,128)(2,1)S(1)}, bf16[2,2,128,128]{3,2,1,0:T(8,128)(2,1)S(1)}, u32[]{:S(2)}, u32[]{:S(2)}) collective-permute-start(bf16[2,2,128,128]{3,2,1,0:T(8,128)(2,1)S(1)} %stack.20), channel_id=1, source_target_pairs={{0,2},{2,0},{1,3},{3,1},{4,6},{6,4},{5,7},{7,5},{8,10},{10,8},{9,1... | collective-permute-start | bytes 393224 | tf_op jit(solution)/shard_map/ppermute | solution.py:15
  29.1 4.1 %dynamic-slice_bitcast_fusion.47 = (bf16[128,512]{1,0:T(8,128)(2,1)}, bf16[128,512]{1,0:T(8,128)(2,1)}, bf16[128,512]{1,0:T(8,128)(2,1)}, bf16[128,512]{1,0:T(8,...) fusion(bf16[8,2,512,512]{3,2,1,0:T(8,128)(2,1)} %param.11, ...), kind=kLoop, calls=%fused_computation.242 | loop fusion | bytes 6291512 | tf_op jit(solution)/shard_map/squeeze | solution.py:68
  33.3 0.6 scatter_fusion.1
  33.9 0.6 gather_fusion.1
  34.5 0.1 select_bitcast_fusion
  34.7 0.1 copy.16
  34.8 0.1 copy.15
  34.9 0.1 fusion.223
  35.1 0.4 collective-permute-start.2
  35.5 4.5 %dynamic-slice_bitcast_fusion.17 = (bf16[512,512]{1,0:T(8,128)(2,1)S(1)}, bf16[512,512]{1,0:T(8,128)(2,1)S(1)}, bf16[512,512]{1,0:T(8,128)(2,1)}, bf16[512,512]{...) fusion(bf16[8,2,512,512]{3,2,1,0:T(8,128)(2,1)} %param.11, ...), kind=kLoop, calls=%fused_computation.192 | loop fusion | bytes 12582960 | tf_op jit(solution)/shard_map/squeeze | solution.py:31
  40.0 0.1 maximum_select_fusion.1
  40.1 1.4 %collective-permute-start.3 = (bf16[2,2,128,512]{3,2,1,0:T(8,128)(2,1)S(1)}, bf16[2,2,128,512]{3,2,1,0:T(8,128)(2,1)}, u32[]{:S(2)}, u32[]{:S(2)}) collective-permute-start(bf16[2,2,128,512]{3,2,1,0:T(8,128)(2,1)S(1)} %maximum_select_fusion.1), channel_id=1, source_target_pairs={{0,2},{2,0},{1,3},{3,1},{4,6},{6,4},{5,7},{7,5},{8,10},{10,8},{9,1... | collective-permute-start | bytes 1572872 | tf_op jit(solution)/shard_map/ppermute | solution.py:15
  41.5 0.7 fusion.255
  42.2 3.4 %fusion.240 = (bf16[512,512]{1,0:T(8,128)(2,1)S(1)}, bf16[512,512]{1,0:T(8,128)(2,1)S(1)}, bf16[512,512]{1,0:T(8,128)(2,1)}, bf16[512,512]{1,0:T(8,128)(2,1)}, b...) fusion(bf16[8,2,512,512]{3,2,1,0:T(8,128)(2,1)S(1)} %bitcast.15, ...), kind=kLoop, calls=%fused_computation.263 | loop fusion | flops 3145728 | bytes 18874420 | tf_op jit(solution)/shard_map/neg | solution.py:32
  45.5 8.9 %collective-permute-done.3 = bf16[2,2,128,512]{3,2,1,0:T(8,128)(2,1)} collective-permute-done((bf16[2,2,128,512]{3,2,1,0:T(8,128)(2,1)S(1)}, bf16[2,2,128,512]{3,2,1,0:T(8,128)(2,1)}, u32[]{:S(2)}, u32[]{:S(2)}) %collective-permute-start.3) | collective-permute-done | bytes 524320 | tf_op jit(solution)/shard_map/ppermute | solution.py:15
  54.4 1.4 %fusion.180 = bf16[2,4,128,512]{3,2,0,1:T(8,128)(2,1)S(1)} fusion(bf16[2,2,128,512]{3,2,1,0:T(8,128)(2,1)S(1)} %maximum_select_fusion.1, bf16[2,2,128,512]{3,2,1,0:T(8,128)(2,1)} %collective-permute-done.3, pred[]{:T(512)S(6)} %eq.8), kind=kLoop, calls=%fused_computation.143 | loop fusion | flops 1572864 | bytes 2097153 | tf_op jit(solution)/shard_map/transpose | solution.py:55
  55.9 0.1 fusion.252
  55.9 0.1 bitcast_negate_fusion
  56.0 0.7 copy-done.36
  56.8 0.1 copy-done.38
  56.8 0.1 copy-done.39
  56.9 0.1 copy-done.40
  57.1 1.2 %convolution_convert_fusion = bf16[512,1024]{1,0:T(8,128)(2,1)S(1)} fusion(bf16[128,512]{1,0:T(8,128)(2,1)S(1)} %copy-done.40, bf16[128,512]{1,0:T(8,128)(2,1)S(1)} %copy-done.36, bf16[128,512]{1,0:T(8,128)(2,1)S(1)} %copy-done.41, bf16[128,512]{1,0:T(8,128)(2,1)S(1)} %copy-done.37, bf16[128,512]{1,0:T(8,128)(2,1)S(1)} %copy-done.42, ...), kind=kOutput, calls=%fused_computation.101 | convolution fusion | flops 1091043328 | bytes 3670016 | tf_op jit(solution)/shard_map/dot_general | solution.py:70
  58.4 0.1 copy-done.19
  58.4 1.6 %fusion.114 = f32[128,1024]{1,0:T(8,128)S(1)} fusion(bf16[512,512]{1,0:T(8,128)(2,1)S(1)} %copy-done.5, bf16[512,512]{1,0:T(8,128)(2,1)S(1)} %copy-done.18, bf16[512,512]{1,0:T(8,128)(2,1)S(1)} %copy-done.19, bf16[512,1024]{1,0:T(8,128)(2,1)S(1)} %convolution_convert_fusion, f32[]{:T(128)} %bitcast.58), kind=kOutput, calls=%fused_computation.110 | convolution fusion | flops 276955136 | bytes 2359300 | tf_op jit(solution)/shard_map/dot_general | solution.py:76
  60.1 1.6 %fusion.111 = f32[128,1024]{1,0:T(8,128)S(1)} fusion(f32[128,1024]{1,0:T(8,128)S(1)} %fusion.114, bf16[512,512]{1,0:T(8,128)(2,1)S(1)} %copy-done.2, bf16[512,512]{1,0:T(8,128)(2,1)S(1)} %copy-done.16, bf16[512,512]{1,0:T(8,128)(2,1)S(1)} %copy-done.17, bf16[512,1024]{1,0:T(8,128)(2,1)S(1)} %convolution_convert_fusion, f32[]{:T(128)} %bitcast.73), kind=kOutput, calls=%fused_computation.109 | convolution fusion | flops 277086208 | bytes 2883588 | tf_op jit(solution)/shard_map/dot_general | solution.py:76
  61.7 1.5 %fusion.105 = f32[128,1024]{1,0:T(8,128)S(1)} fusion(f32[128,1024]{1,0:T(8,128)S(1)} %fusion.111, bf16[512,512]{1,0:T(8,128)(2,1)S(1)} %copy-done.1, bf16[512,512]{1,0:T(8,128)(2,1)S(1)} %copy-done.14, bf16[512,512]{1,0:T(8,128)(2,1)S(1)} %copy-done.15, bf16[512,1024]{1,0:T(8,128)(2,1)S(1)} %convolution_convert_fusion, f32[]{:T(128)} %bitcast.76), kind=kOutput, calls=%fused_computation.107 | convolution fusion | flops 277086208 | bytes 2883588 | tf_op jit(solution)/shard_map/dot_general | solution.py:76
  63.4 1.6 %fusion.99 = f32[128,1024]{1,0:T(8,128)S(1)} fusion(f32[128,1024]{1,0:T(8,128)S(1)} %fusion.105, bf16[512,512]{1,0:T(8,128)(2,1)S(1)} %get-tuple-element.53, bf16[512,512]{1,0:T(8,128)(2,1)S(1)} %copy-done.12, bf16[512,512]{1,0:T(8,128)(2,1)S(1)} %copy-done.13, bf16[512,1024]{1,0:T(8,128)(2,1)S(1)} %convolution_convert_fusion, f32[]{:T(128)} %bitcast.79), kind=kOutput, calls=%fused_computation.105 | convolution fusion | flops 277086208 | bytes 2883588 | tf_op jit(solution)/shard_map/dot_general | solution.py:76
  64.9 3.7 %collective-permute-start.5 = (f32[128,1024]{1,0:T(8,128)S(1)}, f32[128,1024]{1,0:T(8,128)S(1)}, u32[]{:S(2)}, u32[]{:S(2)}) collective-permute-start(f32[128,1024]{1,0:T(8,128)S(1)} %fusion.99), channel_id=1, source_target_pairs={{4,0},{5,1},{6,2},{7,3},{8,4},{9,5},{10,6},{11,7},{12,8},{13,9},{1... | collective-permute-start | bytes 1572872 | tf_op jit(solution)/shard_map/ppermute | solution.py:21
  68.7 1.2 %convolution_convert_fusion.1 = bf16[512,1024]{1,0:T(8,128)(2,1)S(1)} fusion(bf16[128,512]{1,0:T(8,128)(2,1)S(1)} %copy-done.32, bf16[128,512]{1,0:T(8,128)(2,1)S(1)} %copy-done.28, bf16[128,512]{1,0:T(8,128)(2,1)S(1)} %copy-done.33, bf16[128,512]{1,0:T(8,128)(2,1)S(1)} %copy-done.29, bf16[128,512]{1,0:T(8,128)(2,1)S(1)} %copy-done.34, ...), kind=kOutput, calls=%fused_computation.102 | convolution fusion | flops 1091043328 | bytes 3670016 | tf_op jit(solution)/shard_map/dot_general | solution.py:70
  70.0 1.6 %fusion.135 = f32[128,1024]{1,0:T(8,128)S(1)} fusion(bf16[512,512]{1,0:T(8,128)(2,1)S(1)} %get-tuple-element.60, bf16[512,512]{1,0:T(8,128)(2,1)S(1)} %copy-done.10, bf16[512,512]{1,0:T(8,128)(2,1)S(1)} %copy-done.11, bf16[512,1024]{1,0:T(8,128)(2,1)S(1)} %convolution_convert_fusion.1, f32[]{:T(128)} %bitcast.34), kind=kOutput, calls=%fused_computation.117 | convolution fusion | flops 276955136 | bytes 2359300 | tf_op jit(solution)/shard_map/dot_general | solution.py:76
  71.6 1.5 %fusion.132 = f32[128,1024]{1,0:T(8,128)S(1)} fusion(f32[128,1024]{1,0:T(8,128)S(1)} %fusion.135, bf16[512,512]{1,0:T(8,128)(2,1)S(1)} %get-tuple-element.59, bf16[512,512]{1,0:T(8,128)(2,1)S(1)} %copy-done.8, bf16[512,512]{1,0:T(8,128)(2,1)S(1)} %copy-done.9, bf16[512,1024]{1,0:T(8,128)(2,1)S(1)} %convolution_convert_fusion.1, f32[]{:T(128)} %bitcast.49), kind=kOutput, calls=%fused_computation.116 | convolution fusion | flops 277086208 | bytes 2883588 | tf_op jit(solution)/shard_map/dot_general | solution.py:76
  73.2 1.5 %fusion.126 = f32[128,1024]{1,0:T(8,128)S(1)} fusion(f32[128,1024]{1,0:T(8,128)S(1)} %fusion.132, bf16[512,512]{1,0:T(8,128)(2,1)S(1)} %get-tuple-element.58, bf16[512,512]{1,0:T(8,128)(2,1)S(1)} %copy-done.6, bf16[512,512]{1,0:T(8,128)(2,1)S(1)} %copy-done.7, bf16[512,1024]{1,0:T(8,128)(2,1)S(1)} %convolution_convert_fusion.1, f32[]{:T(128)} %bitcast.52), kind=kOutput, calls=%fused_computation.114 | convolution fusion | flops 277086208 | bytes 2883588 | tf_op jit(solution)/shard_map/dot_general | solution.py:76
  74.8 1.6 %fusion.120 = f32[128,1024]{1,0:T(8,128)S(1)} fusion(f32[128,1024]{1,0:T(8,128)S(1)} %fusion.126, bf16[512,512]{1,0:T(8,128)(2,1)S(1)} %get-tuple-element.57, bf16[512,512]{1,0:T(8,128)(2,1)S(1)} %copy-done.3, bf16[512,512]{1,0:T(8,128)(2,1)S(1)} %copy-done.4, bf16[512,1024]{1,0:T(8,128)(2,1)S(1)} %convolution_convert_fusion.1, f32[]{:T(128)} %bitcast.55), kind=kOutput, calls=%fused_computation.112 | convolution fusion | flops 277086208 | bytes 2883588 | tf_op jit(solution)/shard_map/dot_general | solution.py:76
  76.5 1.2 %convolution_convert_fusion.2 = bf16[512,1024]{1,0:T(8,128)(2,1)S(1)} fusion(bf16[128,512]{1,0:T(8,128)(2,1)S(1)} %copy-done.24, bf16[128,512]{1,0:T(8,128)(2,1)S(1)} %copy-done.21, bf16[128,512]{1,0:T(8,128)(2,1)S(1)} %copy-done.25, bf16[128,512]{1,0:T(8,128)(2,1)S(1)} %copy-done.22, bf16[128,512]{1,0:T(8,128)(2,1)S(1)} %copy-done.26, ...), kind=kOutput, calls=%fused_computation.103 | convolution fusion | flops 1091043328 | bytes 3670016 | tf_op jit(solution)/shard_map/dot_general | solution.py:70
  77.7 1.4 %fusion.156 = f32[128,1024]{1,0:T(8,128)S(1)} fusion(bf16[512,512]{1,0:T(8,128)(2,1)S(1)} %get-tuple-element.63, bf16[512,512]{1,0:T(8,128)(2,1)S(1)} %get-tuple-element.46, bf16[512,512]{1,0:T(8,128)(2,1)S(1)} %get-tuple-element.47, bf16[512,1024]{1,0:T(8,128)(2,1)S(1)} %convolution_convert_fusion.2, f32[]{:T(128)} %bitcast), kind=kOutput, calls=%fused_computation.124 | convolution fusion | flops 276955136 | bytes 2359300 | tf_op jit(solution)/shard_map/dot_general | solution.py:76
  79.2 1.4 %fusion.153 = f32[128,1024]{1,0:T(8,128)S(1)} fusion(f32[128,1024]{1,0:T(8,128)S(1)} %fusion.156, bf16[512,512]{1,0:T(8,128)(2,1)S(1)} %get-tuple-element.62, bf16[512,512]{1,0:T(8,128)(2,1)S(1)} %get-tuple-element.44, bf16[512,512]{1,0:T(8,128)(2,1)S(1)} %get-tuple-element.45, bf16[512,1024]{1,0:T(8,128)(2,1)S(1)} %convolution_convert_fusion.2, f32[]{:T(128)} %bitcast.25), kind=kOutput, calls=%fused_computation.123 | convolution fusion | flops 277086208 | bytes 2883588 | tf_op jit(solution)/shard_map/dot_general | solution.py:76
  80.6 1.4 %fusion.147 = f32[128,1024]{1,0:T(8,128)S(1)} fusion(f32[128,1024]{1,0:T(8,128)S(1)} %fusion.153, bf16[512,512]{1,0:T(8,128)(2,1)S(1)} %get-tuple-element.61, bf16[512,512]{1,0:T(8,128)(2,1)S(1)} %get-tuple-element.42, bf16[512,512]{1,0:T(8,128)(2,1)S(1)} %get-tuple-element.43, bf16[512,1024]{1,0:T(8,128)(2,1)S(1)} %convolution_convert_fusion.2, f32[]{:T(128)} %bitcast.28), kind=kOutput, calls=%fused_computation.121 | convolution fusion | flops 277086208 | bytes 2883588 | tf_op jit(solution)/shard_map/dot_general | solution.py:76
  82.0 9.8 %collective-permute-done.4 = f32[128,1024]{1,0:T(8,128)S(1)} collective-permute-done((f32[128,1024]{1,0:T(8,128)S(1)}, f32[128,1024]{1,0:T(8,128)S(1)}, u32[]{:S(2)}, u32[]{:S(2)}) %collective-permute-start.4) | collective-permute-done | bytes 524320 | tf_op jit(solution)/shard_map/ppermute | solution.py:21
  91.9 1.5 %fusion.162 = f32[128,1024]{1,0:T(8,128)S(1)} fusion(f32[128,1024]{1,0:T(8,128)S(1)} %collective-permute-done.5, f32[128,1024]{1,0:T(8,128)S(1)} %collective-permute-done.4, f32[128,1024]{1,0:T(8,128)S(1)} %fusion.147, bf16[512,512]{1,0:T(8,128)(2,1)S(1)} %get-tuple-element.52, bf16[512,512]{1,0:T(8,128)(2,1)S(1)} %get-tuple-element.6, ...), kind=kOutput, calls=%fused_computation.126 | convolution fusion | flops 277348352 | bytes 3932164 | tf_op jit(solution)/shard_map/dot_general | solution.py:76
  93.3 0.8 copy.20
  (109 shorter events, 0.6 us)
Async XLA Ops:
  0.0 25.9 %copy-start.47 = (s32[2]{0:T(128)S(1)}, s32[2]{0:T(128)}, u32[]{:S(2)}) copy-start(s32[2]{0:T(128)} %constant.315) | copy-start | bytes 28
  0.0 2.6 %copy-start.44 = (s32[3,4]{1,0:T(4,128)S(1)}, s32[3,4]{1,0:T(4,128)}, u32[]{:S(2)}) copy-start(s32[3,4]{1,0:T(4,128)} %param.12) | copy-start | bytes 148
  2.1 23.8 %collective-permute-start = (bf16[2,2,128,128]{3,2,1,0:T(8,128)(2,1)S(1)}, bf16[2,2,128,128]{3,2,1,0:T(8,128)(2,1)S(1)}, u32[]{:S(2)}, u32[]{:S(2)}) collective-permute-start(bf16[2,2,128,128]{3,2,1,0:T(8,128)(2,1)S(1)} %pad_maximum_fusion.1), channel_id=1, source_target_pairs={{0,1},{1,0},{2,3},{3,2},{4,5},{5,4},{6,7},{7,6},{8,9},{9,8},{10,11... | collective-permute-start | bytes 393224 | tf_op jit(solution)/shard_map/ppermute | solution.py:15
  26.6 6.7 %copy-start.46 = (s32[2]{0:T(128)S(1)}, s32[2]{0:T(128)}, u32[]{:S(2)}) copy-start(s32[2]{0:T(128)} %constant.316) | copy-start | bytes 28
  26.6 6.7 %collective-permute-start.1 = (bf16[2,2,128,128]{3,2,1,0:T(8,128)(2,1)S(1)}, bf16[2,2,128,128]{3,2,1,0:T(8,128)(2,1)S(1)}, u32[]{:S(2)}, u32[]{:S(2)}) collective-permute-start(bf16[2,2,128,128]{3,2,1,0:T(8,128)(2,1)S(1)} %stack.20), channel_id=1, source_target_pairs={{0,2},{2,0},{1,3},{3,1},{4,6},{6,4},{5,7},{7,5},{8,10},{10,8},{9,1... | collective-permute-start | bytes 393224 | tf_op jit(solution)/shard_map/ppermute | solution.py:15
  33.3 1.6 %copy-start = (bf16[2,128,512]{2,1,0:T(8,128)(2,1)S(1)}, bf16[2,128,512]{2,1,0:T(8,128)(2,1)}, u32[]{:S(2)}) copy-start(bf16[2,128,512]{2,1,0:T(8,128)(2,1)} %param.10) | copy-start | bytes 786436
  34.9 7.2 %slice-start = ((s8[8388608]{0:T(1024)(128)(4,1)}), s8[4194304]{0:T(1024)(128)(4,1)S(1)}, s32[]{:S(2)}) async-start(s8[8388608]{0:T(1024)(128)(4,1)} %bitcast.158), calls=%async_computation | async-start | bytes 8388608
  35.1 6.4 %copy-start.45 = (f32[3,4]{1,0:T(4,128)S(1)}, f32[3,4]{1,0:T(4,128)}, u32[]{:S(2)}) copy-start(f32[3,4]{1,0:T(4,128)} %param.13) | copy-start | bytes 148
  35.1 7.1 %slice-start.1 = ((s8[8388608]{0:T(1024)(128)(4,1)}), s8[4194304]{0:T(1024)(128)(4,1)S(1)}, s32[]{:S(2)}) async-start(s8[8388608]{0:T(1024)(128)(4,1)} %bitcast.158), calls=%async_computation.1 | async-start | bytes 8388608
  35.1 4.9 %collective-permute-start.2 = (bf16[1,2,128,512]{3,2,1,0:T(8,128)(2,1)S(1)}, bf16[1,2,128,512]{3,2,1,0:T(8,128)(2,1)S(1)}, u32[]{:S(2)}, u32[]{:S(2)}) collective-permute-start(bf16[1,2,128,512]{3,2,1,0:T(8,128)(2,1)S(1)} %pad_maximum_fusion), channel_id=1, source_target_pairs={{0,1},{1,0},{2,3},{3,2},{4,5},{5,4},{6,7},{7,6},{8,9},{9,8},{10,11... | collective-permute-start | bytes 786440 | tf_op jit(solution)/shard_map/ppermute | solution.py:15
  40.1 14.3 %collective-permute-start.3 = (bf16[2,2,128,512]{3,2,1,0:T(8,128)(2,1)S(1)}, bf16[2,2,128,512]{3,2,1,0:T(8,128)(2,1)}, u32[]{:S(2)}, u32[]{:S(2)}) collective-permute-start(bf16[2,2,128,512]{3,2,1,0:T(8,128)(2,1)S(1)} %maximum_select_fusion.1), channel_id=1, source_target_pairs={{0,2},{2,0},{1,3},{3,1},{4,6},{6,4},{5,7},{7,5},{8,10},{10,8},{9,1... | collective-permute-start | bytes 1572872 | tf_op jit(solution)/shard_map/ppermute | solution.py:15
  57.1 1.3 %copy-start.5 = (bf16[512,512]{1,0:T(8,128)(2,1)S(1)}, bf16[512,512]{1,0:T(8,128)(2,1)}, u32[]{:S(2)}) copy-start(bf16[512,512]{1,0:T(8,128)(2,1)} %get-tuple-element.56) | copy-start | bytes 1572868
  57.1 1.3 %copy-start.18 = (bf16[512,512]{1,0:T(8,128)(2,1)S(1)}, bf16[512,512]{1,0:T(8,128)(2,1)}, u32[]{:S(2)}) copy-start(bf16[512,512]{1,0:T(8,128)(2,1)} %get-tuple-element.32) | copy-start | bytes 1572868
  57.1 1.4 %copy-start.19 = (bf16[512,512]{1,0:T(8,128)(2,1)S(1)}, bf16[512,512]{1,0:T(8,128)(2,1)}, u32[]{:S(2)}) copy-start(bf16[512,512]{1,0:T(8,128)(2,1)} %get-tuple-element.33) | copy-start | bytes 1572868
  58.4 1.6 %copy-start.2 = (bf16[512,512]{1,0:T(8,128)(2,1)S(1)}, bf16[512,512]{1,0:T(8,128)(2,1)}, u32[]{:S(2)}) copy-start(bf16[512,512]{1,0:T(8,128)(2,1)} %get-tuple-element.55) | copy-start | bytes 1572868
  58.4 1.6 %copy-start.16 = (bf16[512,512]{1,0:T(8,128)(2,1)S(1)}, bf16[512,512]{1,0:T(8,128)(2,1)}, u32[]{:S(2)}) copy-start(bf16[512,512]{1,0:T(8,128)(2,1)} %get-tuple-element.30) | copy-start | bytes 1572868
  58.4 1.6 %copy-start.17 = (bf16[512,512]{1,0:T(8,128)(2,1)S(1)}, bf16[512,512]{1,0:T(8,128)(2,1)}, u32[]{:S(2)}) copy-start(bf16[512,512]{1,0:T(8,128)(2,1)} %get-tuple-element.31) | copy-start | bytes 1572868
  60.1 1.6 %copy-start.1 = (bf16[512,512]{1,0:T(8,128)(2,1)S(1)}, bf16[512,512]{1,0:T(8,128)(2,1)}, u32[]{:S(2)}) copy-start(bf16[512,512]{1,0:T(8,128)(2,1)} %get-tuple-element.54) | copy-start | bytes 1572868
  60.1 1.6 %copy-start.14 = (bf16[512,512]{1,0:T(8,128)(2,1)S(1)}, bf16[512,512]{1,0:T(8,128)(2,1)}, u32[]{:S(2)}) copy-start(bf16[512,512]{1,0:T(8,128)(2,1)} %get-tuple-element.50) | copy-start | bytes 1572868
  60.1 1.6 %copy-start.15 = (bf16[512,512]{1,0:T(8,128)(2,1)S(1)}, bf16[512,512]{1,0:T(8,128)(2,1)}, u32[]{:S(2)}) copy-start(bf16[512,512]{1,0:T(8,128)(2,1)} %get-tuple-element.51) | copy-start | bytes 1572868
  61.7 1.6 %copy-start.12 = (bf16[512,512]{1,0:T(8,128)(2,1)S(1)}, bf16[512,512]{1,0:T(8,128)(2,1)}, u32[]{:S(2)}) copy-start(bf16[512,512]{1,0:T(8,128)(2,1)} %get-tuple-element.48) | copy-start | bytes 1572868
  61.7 1.6 %copy-start.13 = (bf16[512,512]{1,0:T(8,128)(2,1)S(1)}, bf16[512,512]{1,0:T(8,128)(2,1)}, u32[]{:S(2)}) copy-start(bf16[512,512]{1,0:T(8,128)(2,1)} %get-tuple-element.49) | copy-start | bytes 1572868
  63.3 5.3 %copy-start.28 = (bf16[128,512]{1,0:T(8,128)(2,1)S(1)}, bf16[128,512]{1,0:T(8,128)(2,1)}, u32[]{:S(2)}) copy-start(bf16[128,512]{1,0:T(8,128)(2,1)} %get-tuple-element.69) | copy-start | bytes 393220
  63.3 5.3 %copy-start.29 = (bf16[128,512]{1,0:T(8,128)(2,1)S(1)}, bf16[128,512]{1,0:T(8,128)(2,1)}, u32[]{:S(2)}) copy-start(bf16[128,512]{1,0:T(8,128)(2,1)} %get-tuple-element.70) | copy-start | bytes 393220
  63.3 5.3 %copy-start.30 = (bf16[128,512]{1,0:T(8,128)(2,1)S(1)}, bf16[128,512]{1,0:T(8,128)(2,1)}, u32[]{:S(2)}) copy-start(bf16[128,512]{1,0:T(8,128)(2,1)} %get-tuple-element.71) | copy-start | bytes 393220
  63.3 5.3 %copy-start.31 = (bf16[128,512]{1,0:T(8,128)(2,1)S(1)}, bf16[128,512]{1,0:T(8,128)(2,1)}, u32[]{:S(2)}) copy-start(bf16[128,512]{1,0:T(8,128)(2,1)} %get-tuple-element.72) | copy-start | bytes 393220
  63.3 5.3 %copy-start.32 = (bf16[128,512]{1,0:T(8,128)(2,1)S(1)}, bf16[128,512]{1,0:T(8,128)(2,1)}, u32[]{:S(2)}) copy-start(bf16[128,512]{1,0:T(8,128)(2,1)} %get-tuple-element.80) | copy-start | bytes 393220
  63.3 5.3 %copy-start.33 = (bf16[128,512]{1,0:T(8,128)(2,1)S(1)}, bf16[128,512]{1,0:T(8,128)(2,1)}, u32[]{:S(2)}) copy-start(bf16[128,512]{1,0:T(8,128)(2,1)} %get-tuple-element.81) | copy-start | bytes 393220
  63.4 5.3 %copy-start.34 = (bf16[128,512]{1,0:T(8,128)(2,1)S(1)}, bf16[128,512]{1,0:T(8,128)(2,1)}, u32[]{:S(2)}) copy-start(bf16[128,512]{1,0:T(8,128)(2,1)} %get-tuple-element.82) | copy-start | bytes 393220
  63.4 5.3 %copy-start.35 = (bf16[128,512]{1,0:T(8,128)(2,1)S(1)}, bf16[128,512]{1,0:T(8,128)(2,1)}, u32[]{:S(2)}) copy-start(bf16[128,512]{1,0:T(8,128)(2,1)} %get-tuple-element.83) | copy-start | bytes 393220
  64.9 17.1 %collective-permute-start.5 = (f32[128,1024]{1,0:T(8,128)S(1)}, f32[128,1024]{1,0:T(8,128)S(1)}, u32[]{:S(2)}, u32[]{:S(2)}) collective-permute-start(f32[128,1024]{1,0:T(8,128)S(1)} %fusion.99), channel_id=1, source_target_pairs={{4,0},{5,1},{6,2},{7,3},{8,4},{9,5},{10,6},{11,7},{12,8},{13,9},{1... | collective-permute-start | bytes 1572872 | tf_op jit(solution)/shard_map/ppermute | solution.py:21
  68.7 1.3 %copy-start.10 = (bf16[512,512]{1,0:T(8,128)(2,1)S(1)}, bf16[512,512]{1,0:T(8,128)(2,1)}, u32[]{:S(2)}) copy-start(bf16[512,512]{1,0:T(8,128)(2,1)} %get-tuple-element.40) | copy-start | bytes 1572868
  68.7 1.3 %copy-start.11 = (bf16[512,512]{1,0:T(8,128)(2,1)S(1)}, bf16[512,512]{1,0:T(8,128)(2,1)}, u32[]{:S(2)}) copy-start(bf16[512,512]{1,0:T(8,128)(2,1)} %get-tuple-element.41) | copy-start | bytes 1572868
  70.0 1.6 %copy-start.8 = (bf16[512,512]{1,0:T(8,128)(2,1)S(1)}, bf16[512,512]{1,0:T(8,128)(2,1)}, u32[]{:S(2)}) copy-start(bf16[512,512]{1,0:T(8,128)(2,1)} %get-tuple-element.38) | copy-start | bytes 1572868
  70.0 1.6 %copy-start.9 = (bf16[512,512]{1,0:T(8,128)(2,1)S(1)}, bf16[512,512]{1,0:T(8,128)(2,1)}, u32[]{:S(2)}) copy-start(bf16[512,512]{1,0:T(8,128)(2,1)} %get-tuple-element.39) | copy-start | bytes 1572868
  71.6 1.5 %copy-start.6 = (bf16[512,512]{1,0:T(8,128)(2,1)S(1)}, bf16[512,512]{1,0:T(8,128)(2,1)}, u32[]{:S(2)}) copy-start(bf16[512,512]{1,0:T(8,128)(2,1)} %get-tuple-element.36) | copy-start | bytes 1572868
  71.6 1.5 %copy-start.7 = (bf16[512,512]{1,0:T(8,128)(2,1)S(1)}, bf16[512,512]{1,0:T(8,128)(2,1)}, u32[]{:S(2)}) copy-start(bf16[512,512]{1,0:T(8,128)(2,1)} %get-tuple-element.37) | copy-start | bytes 1572868
  73.2 1.5 %copy-start.3 = (bf16[512,512]{1,0:T(8,128)(2,1)S(1)}, bf16[512,512]{1,0:T(8,128)(2,1)}, u32[]{:S(2)}) copy-start(bf16[512,512]{1,0:T(8,128)(2,1)} %get-tuple-element.34) | copy-start | bytes 1572868
  73.2 1.5 %copy-start.4 = (bf16[512,512]{1,0:T(8,128)(2,1)S(1)}, bf16[512,512]{1,0:T(8,128)(2,1)}, u32[]{:S(2)}) copy-start(bf16[512,512]{1,0:T(8,128)(2,1)} %get-tuple-element.35) | copy-start | bytes 1572868
  74.7 1.7 %copy-start.20 = (bf16[128,512]{1,0:T(8,128)(2,1)S(1)}, bf16[128,512]{1,0:T(8,128)(2,1)}, u32[]{:S(2)}) copy-start(bf16[128,512]{1,0:T(8,128)(2,1)} %get-tuple-element.64) | copy-start | bytes 393220
  74.7 1.7 %copy-start.21 = (bf16[128,512]{1,0:T(8,128)(2,1)S(1)}, bf16[128,512]{1,0:T(8,128)(2,1)}, u32[]{:S(2)}) copy-start(bf16[128,512]{1,0:T(8,128)(2,1)} %get-tuple-element.73) | copy-start | bytes 393220
  74.7 1.7 %copy-start.22 = (bf16[128,512]{1,0:T(8,128)(2,1)S(1)}, bf16[128,512]{1,0:T(8,128)(2,1)}, u32[]{:S(2)}) copy-start(bf16[128,512]{1,0:T(8,128)(2,1)} %get-tuple-element.74) | copy-start | bytes 393220
  74.7 1.7 %copy-start.23 = (bf16[128,512]{1,0:T(8,128)(2,1)S(1)}, bf16[128,512]{1,0:T(8,128)(2,1)}, u32[]{:S(2)}) copy-start(bf16[128,512]{1,0:T(8,128)(2,1)} %get-tuple-element.75) | copy-start | bytes 393220
  74.7 1.7 %copy-start.24 = (bf16[128,512]{1,0:T(8,128)(2,1)S(1)}, bf16[128,512]{1,0:T(8,128)(2,1)}, u32[]{:S(2)}) copy-start(bf16[128,512]{1,0:T(8,128)(2,1)} %get-tuple-element.84) | copy-start | bytes 393220
  74.7 1.7 %copy-start.25 = (bf16[128,512]{1,0:T(8,128)(2,1)S(1)}, bf16[128,512]{1,0:T(8,128)(2,1)}, u32[]{:S(2)}) copy-start(bf16[128,512]{1,0:T(8,128)(2,1)} %get-tuple-element.85) | copy-start | bytes 393220
  74.8 1.7 %copy-start.26 = (bf16[128,512]{1,0:T(8,128)(2,1)S(1)}, bf16[128,512]{1,0:T(8,128)(2,1)}, u32[]{:S(2)}) copy-start(bf16[128,512]{1,0:T(8,128)(2,1)} %get-tuple-element.86) | copy-start | bytes 393220
  74.8 1.7 %copy-start.27 = (bf16[128,512]{1,0:T(8,128)(2,1)S(1)}, bf16[128,512]{1,0:T(8,128)(2,1)}, u32[]{:S(2)}) copy-start(bf16[128,512]{1,0:T(8,128)(2,1)} %get-tuple-element.87) | copy-start | bytes 393220
  76.3 15.5 %collective-permute-start.4 = (f32[128,1024]{1,0:T(8,128)S(1)}, f32[128,1024]{1,0:T(8,128)S(1)}, u32[]{:S(2)}, u32[]{:S(2)}) collective-permute-start(f32[128,1024]{1,0:T(8,128)S(1)} %fusion.120), channel_id=1, source_target_pairs={{12,0},{13,1},{14,2},{15,3},{0,4},{1,5},{2,6},{3,7},{4,8},{5,9},{6... | collective-permute-start | bytes 1572872 | tf_op jit(solution)/shard_map/ppermute | solution.py:21
  (8 other events, 8.7 us)
where the time goes:
time: 95 us; the launch traced here: 94.2 us
  between operations  23.5 us (25%)
  matrix products  21.8 us (23%)
  waiting for transfers between devices  18.7 us (20%)
  local copies, waits for them, and re-layouts  16.2 us (17%)
  starting transfers between devices  8.67 us (9%)
  other arithmetic  5.21 us (5%)
    dot_general x12, matrix products, stop_term(): lax.dot_general(product, right_list[mode_index], (((1,), (1,)), ((), ()))...  18.1 us
    ppermute x2, waiting for transfers between devices, passed_along(): return lax.ppermute(block, axis, route)  9.85 us
    ppermute x4, waiting for transfers between devices, partner(): return lax.ppermute(block, axis, route)  8.89 us
    ppermute x4, starting transfers between devices, partner(): return lax.ppermute(block, axis, route)  4.9 us
    squeeze x1, local copies, waits for them, and re-layouts, stack_coupling(): upper_half = jnp.concatenate([coupling[0], coupling[1]], axis=1)  4.48 us
    squeeze x1, local copies, waits for them, and re-layouts, stop_term(): coupled_rows[0]  4.12 us
    ppermute x2, starting transfers between devices, passed_along(): return lax.ppermute(block, axis, route)  3.77 us
    dot_general x3, matrix products, stop_term(): jnp.dot(jnp.concatenate(left_list, axis=0), stacked, preferred_element_ty...  3.74 us
  transfers between devices with their start and end apart: 6, of which 2 were waited for; matrix products, arithmetic and copies ran while one was open for 28% of the time, Pallas kernels for 0%

commit v1 on v0

v1 whole, which is shorter than its diff:
```python
import functools

import jax
import jax.numpy as jnp
from jax import lax
from jax.experimental import pallas as pl
from jax.experimental.pallas import tpu as pltpu
from jax.sharding import PartitionSpec as P

MESH = pl.DeviceIdType.MESH
NT = (((1,), (1,)), ((), ()))


def kernel(
    dims, green, couplings, modes, weights, out,
    gathered, bank, left, rows_stack, product, own, outgoing, incoming,
    own_sem, bank_sem, pair_sems, chip_sems, relay_sems, term_sems,
):
    mom_size, group, tile, order, bank_size, stops, mode_count, chunk = dims
    reach = (stops - 1) // 2
    chips = group // 2
    me = lax.axis_index("mom")
    member = lax.rem(me, group)
    base = me - member
    core = lax.rem(member, 2)
    chip = member // 2
    mate = base + member + 1 - 2 * core

    def at(position):
        return {"mom": position}

    others = [base + lax.rem(chip + d, chips) * 2 + core for d in range(1, chips)]
    shifts = [s for s in range(stops) if s != reach]
    targets = [lax.rem(me + (s - reach) * group + mom_size, mom_size) for s in shifts]

    own_copy = pltpu.make_async_copy(green, gathered.at[member], own_sem)
    own_copy.start()
    loads = []
    for b in range(bank_size):
        for part in range(2):
            load = pltpu.make_async_copy(
                couplings.at[b, part],
                bank.at[b, :, pl.ds(part * order, order)],
                bank_sem.at[b, part],
            )
            load.start()
            loads.append(load)

    barrier = pltpu.get_barrier_semaphore()
    neighbours = [mate] + others + targets
    for neighbour in neighbours:
        pl.semaphore_signal(barrier, inc=1, device_id=at(neighbour), device_id_type=MESH)
    pl.semaphore_wait(barrier, len(neighbours))

    def remote(src, dst, sems, to):
        return pltpu.make_async_remote_copy(
            src_ref=src, dst_ref=dst, send_sem=sems.at[0], recv_sem=sems.at[1],
            device_id=at(to), device_id_type=MESH,
        )

    chip_copies = []
    for part in range(2):
        for d, other in enumerate(others):
            copy = remote(
                green.at[part], gathered.at[member, part], chip_sems.at[d, part], other
            )
            copy.start()
            chip_copies.append((d, part, copy))
    pair_copy = remote(green, gathered.at[member], pair_sems, mate)
    pair_copy.start()
    relays = []
    for d, part, copy in chip_copies:
        source = lax.rem(chip + chips - (d + 1), chips) * 2 + core
        copy.wait_recv()
        relay = remote(
            gathered.at[source, part], gathered.at[source, part], relay_sems.at[d, part], mate
        )
        relay.start()
        relays.append(relay)

    scale = [
        [
            sum(
                jnp.where(modes[s, m] == b, weights[s, m], jnp.float32(0.0))
                for m in range(mode_count)
            )
            for b in range(bank_size)
        ]
        for s in range(stops)
    ]
    for load in loads:
        load.wait()
    for b in range(bank_size):
        left[pl.ds(b * tile, tile), :] = bank[b, pl.ds(pl.multiple_of(member * tile, tile), tile), :]
    own_copy.wait()
    pair_copy.wait_recv()
    for relay in relays:
        relay.wait_recv()

    for j in range(group):
        columns = pl.ds(j * tile, tile)
        mirror = [
            jnp.concatenate(
                [gathered[i, part, :, columns].T for i in range(group)], axis=1
            ).astype(jnp.float32)
            for part in range(2)
        ]
        spec_real = -(gathered[j, 1].astype(jnp.float32) + mirror[1])
        spec_imag = gathered[j, 0].astype(jnp.float32) - mirror[0]
        spec_real = spec_real.astype(jnp.bfloat16)
        spec_imag = spec_imag.astype(jnp.bfloat16)
        rows_stack[pl.ds(2 * j * tile, tile), pl.ds(0, order)] = spec_real
        rows_stack[pl.ds(2 * j * tile, tile), pl.ds(order, order)] = spec_imag
        rows_stack[pl.ds((2 * j + 1) * tile, tile), pl.ds(0, order)] = -spec_imag
        rows_stack[pl.ds((2 * j + 1) * tile, tile), pl.ds(order, order)] = spec_real
        both = lax.dot_general(
            left[...], rows_stack[pl.ds(2 * j * tile, 2 * tile), :], NT,
            preferred_element_type=jnp.float32,
        ).astype(jnp.bfloat16)
        for b in range(bank_size):
            block = both[b * tile : (b + 1) * tile]
            real, imag = block[:, :tile], block[:, tile:]
            product[b, pl.ds(0, tile), pl.ds(j * tile, tile)] = real
            product[b, pl.ds(0, tile), pl.ds(order + j * tile, tile)] = imag
            product[b, pl.ds(tile, tile), pl.ds(j * tile, tile)] = imag
            product[b, pl.ds(tile, tile), pl.ds(order + j * tile, tile)] = -real

    term_copies = []
    for c in range(order // chunk):
        terms = [
            lax.dot_general(
                product[b], bank[b, pl.ds(c * chunk, chunk), :], NT,
                preferred_element_type=jnp.float32,
            )
            for b in range(bank_size)
        ]
        for index, s in enumerate(shifts):
            outgoing[index, c] = sum(
                scale[s][b] * terms[b] for b in range(bank_size)
            ).astype(jnp.bfloat16)
            copy = remote(
                outgoing.at[index, c], incoming.at[index, c], term_sems.at[index, c],
                targets[index],
            )
            copy.start()
            term_copies.append(copy)
        own[c] = sum(scale[reach][b] * terms[b] for b in range(bank_size))

    for c in range(order // chunk):
        total = own[c]
        for index in range(len(shifts)):
            term_copies[c * len(shifts) + index].wait_recv()
            total = total + incoming[index, c].astype(jnp.float32)
        out[0, :, pl.ds(c * chunk, chunk)] = total[:tile]
        out[1, :, pl.ds(c * chunk, chunk)] = total[tile:]

    for _, _, copy in chip_copies:
        copy.wait_send()
    pair_copy.wait_send()
    for relay in relays:
        relay.wait_send()
    for copy in term_copies:
        copy.wait_send()


def body(green_function, couplings, phonon_modes, weights):
    _, tile, order = green_function.shape
    group = order // tile
    chips = group // 2
    bank_size = couplings.shape[0]
    stops, mode_count = phonon_modes.shape
    mom_size = lax.axis_size("mom")
    chunk = min(2 * tile, order)
    chunks = order // chunk
    dims = (mom_size, group, tile, order, bank_size, stops, mode_count, chunk)
    bf16, f32 = jnp.bfloat16, jnp.float32
    flops = 8 * bank_size * tile * order * order * 2
    return pl.pallas_call(
        functools.partial(kernel, dims),
        out_shape=jax.ShapeDtypeStruct((2, tile, order), f32),
        in_specs=[
            pl.BlockSpec(memory_space=pl.ANY),
            pl.BlockSpec(memory_space=pl.ANY),
            pl.BlockSpec(memory_space=pltpu.SMEM),
            pl.BlockSpec(memory_space=pltpu.SMEM),
        ],
        out_specs=pl.BlockSpec(memory_space=pltpu.VMEM),
        scratch_shapes=[
            pltpu.VMEM((group, 2, tile, order), bf16),
            pltpu.VMEM((bank_size, order, 2 * order), bf16),
            pltpu.VMEM((bank_size * tile, 2 * order), bf16),
            pltpu.VMEM((2 * order, 2 * order), bf16),
            pltpu.VMEM((bank_size, 2 * tile, 2 * order), bf16),
            pltpu.VMEM((chunks, 2 * tile, chunk), f32),
            pltpu.VMEM((stops - 1, chunks, 2 * tile, chunk), bf16),
            pltpu.VMEM((stops - 1, chunks, 2 * tile, chunk), bf16),
            pltpu.SemaphoreType.DMA,
            pltpu.SemaphoreType.DMA((bank_size, 2)),
            pltpu.SemaphoreType.DMA((2,)),
            pltpu.SemaphoreType.DMA((max(chips - 1, 1), 2, 2)),
            pltpu.SemaphoreType.DMA((max(chips - 1, 1), 2, 2)),
            pltpu.SemaphoreType.DMA((stops - 1, chunks, 2)),
        ],
        compiler_params=pltpu.CompilerParams(
            collective_id=0, has_side_effects=True, vmem_limit_bytes=48 * 2**20
        ),
        cost_estimate=pl.CostEstimate(flops=flops, bytes_accessed=10 * 2**20, transcendentals=0),
    )(green_function, couplings, phonon_modes, weights)


def solution(mesh):
    in_specs = (P(None, ("grp", "mom"), None), P(), P(), P())
    out_specs = P(None, ("grp", "mom"), None)
    return jax.shard_map(body, mesh=mesh, in_specs=in_specs, out_specs=out_specs, check_vma=False)
```

time: 95 us -> 34.6 us (0.36)
  Pallas kernels: 0 us -> 31.3 us
  between operations: 23.5 us -> 0.01 us
  matrix products: 21.8 us -> 0 us
  waiting for transfers between devices: 18.7 us -> 0 us
  local copies, waits for them, and re-layouts: 16.2 us -> 3.11 us
  starting transfers between devices: 8.67 us -> 0 us
  other arithmetic: 5.21 us -> 0 us
    pallas_call x0 -> x1, Pallas kernels: none -> 31.3 us  [body(): pl.pallas_call(functools.partial(kernel, dims), out_shape=jax.ShapeDtypeS...]
    dot_general x15 -> x0, matrix products: 21.8 us -> none  [the longest x12 18.1 us: stop_term(): lax.dot_general(product, right_list[mode_index], (((1,), (1,)), ((), ()))...]
    ppermute x6 -> x0, waiting for transfers between devices: 18.7 us -> none  [the longest x2 9.85 us: passed_along(): return lax.ppermute(block, axis, route)]
    ppermute x6 -> x0, starting transfers between devices: 8.67 us -> none  [the longest x4 4.9 us: partner(): return lax.ppermute(block, axis, route)]
    squeeze x2 -> x0, local copies, waits for them, and re-layouts: 8.6 us -> none  [the longest x1 4.48 us: stack_coupling(): upper_half = jnp.concatenate([coupling[0], coupling[1]], axis=1)]
    neg x2 -> x0, other arithmetic: 3.45 us -> none  [the longest x1 3.38 us: stack_coupling(): lower_half = jnp.concatenate([-coupling[1], coupling[0]], axis=1)]
    slice x5 -> x0, local copies, waits for them, and re-layouts: 1.47 us -> none  [the longest x1 0.69 us: stop_term(): weighted = weights[stop_index, mode_index] * contribution]
    transpose x2 -> x0, other arithmetic: 1.46 us -> none  [the longest x1 1.37 us: as_slab(): row_blocks.transpose(1, 0, 2, 3)]
  transfers between devices with their start and end apart: 6 -> 0, of which waited for: 2 -> 0; matrix products, arithmetic and copies ran while one was open for 28% -> 0% of each run, Pallas kernels for 0% -> 0%
where the time goes in v1:
time: 34.6 us; the launch traced here: 34.4 us
  Pallas kernels  31.3 us (90%)
  local copies, waits for them, and re-layouts  3.11 us (9%)
    pallas_call x1, Pallas kernels, body(): pl.pallas_call(functools.partial(kernel, dims), out_shape=jax.ShapeDtypeS...  31.3 us
    unnamed x7, local copies, waits for them, and re-layouts  3.11 us

profile of v1, /device:TPU:0, one launch (start us, length us, event | category | flops | bytes accessed | tf_op | source)
XLA Modules:
  0.0 34.4 jit_solution(15566690094187934842)
XLA Ops:
  0.0 0.0 copy-start
  0.0 0.9 %copy-done = bf16[2,128,512]{2,1,0:T(8,128)(2,1)S(1)} copy-done((bf16[2,128,512]{2,1,0:T(8,128)(2,1)S(1)}, bf16[2,128,512]{2,1,0:T(8,128)(2,1)}, u32[]{:S(2)}) %copy-start) | copy-done | bytes 262168
  1.0 0.0 copy-start.1
  1.0 0.7 %copy-done.1 = s32[3,4]{1,0:T(4,128)S(1)} copy-done((s32[3,4]{1,0:T(4,128)S(1)}, s32[3,4]{1,0:T(4,128)}, u32[]{:S(2)}) %copy-start.1) | copy-done | bytes 72
  1.6 0.0 copy-start.2
  1.6 0.7 %copy-done.2 = f32[3,4]{1,0:T(4,128)S(1)} copy-done((f32[3,4]{1,0:T(4,128)S(1)}, f32[3,4]{1,0:T(4,128)}, u32[]{:S(2)}) %copy-start.2) | copy-done | bytes 72
  2.3 31.3 %shard_map.46 = f32[2,128,512]{2,1,0:T(8,128)S(1)} custom-call(bf16[2,128,512]{2,1,0:T(8,128)(2,1)S(1)} %copy-done, bf16[8,2,512,512]{3,2,1,0:T(8,128)(2,1)} %couplings.1, s32[3,4]{1,0:T(4,128)S(1)} %copy-done.1, f32[3,4]{1,0:T(4,128)S(1)} %copy-done.2), custom_call_target="tpu_custom_call" | custom-call | flops 4294967296 | bytes 10485760 | tf_op jit(solution)/shard_map/pallas_call | solution.py:178
  33.6 0.8 %copy.6 = f32[2,128,512]{2,1,0:T(8,128)} copy(f32[2,128,512]{2,1,0:T(8,128)S(1)} %shard_map.46) | data formatting | bytes 1048576
Async XLA Ops:
  0.0 0.9 %copy-start = (bf16[2,128,512]{2,1,0:T(8,128)(2,1)S(1)}, bf16[2,128,512]{2,1,0:T(8,128)(2,1)}, u32[]{:S(2)}) copy-start(bf16[2,128,512]{2,1,0:T(8,128)(2,1)} %green.1) | copy-start | bytes 786436
  1.0 0.7 %copy-start.1 = (s32[3,4]{1,0:T(4,128)S(1)}, s32[3,4]{1,0:T(4,128)}, u32[]{:S(2)}) copy-start(s32[3,4]{1,0:T(4,128)} %modes.1) | copy-start | bytes 148
  1.6 0.7 %copy-start.2 = (f32[3,4]{1,0:T(4,128)S(1)}, f32[3,4]{1,0:T(4,128)}, u32[]{:S(2)}) copy-start(f32[3,4]{1,0:T(4,128)} %weights.1) | copy-start | bytes 148

commit v2 on v1

v2 whole, which is shorter than its diff:
```python
import functools

import jax
import jax.numpy as jnp
from jax import lax
from jax.experimental import pallas as pl
from jax.experimental.pallas import tpu as pltpu
from jax.sharding import PartitionSpec as P

MESH = pl.DeviceIdType.MESH
NT = (((1,), (1,)), ((), ()))


def kernel(
    dims, green, couplings, modes_hbm, weights_hbm, out,
    modes, weights, gathered, bank, left, rows_stack, product,
    own, outgoing, incoming, mate_incoming, mirror_out, mirror_in,
    small_sems, bank_sem, pair_sems, chip_sems, relay_sems, term_sems, mate_term_sems,
    mirror_sems,
):
    mom_size, group, tile, order, bank_size, stops, mode_count = dims
    f32, bf16 = jnp.float32, jnp.bfloat16
    reach = (stops - 1) // 2
    chips = group // 2
    wide = 2 * tile
    me = lax.axis_index("mom")
    member = lax.rem(me, group)
    base = me - member
    core = lax.rem(member, 2)
    chip = member // 2
    mate = base + chip * 2 + 1 - core

    def at(position):
        return {"mom": position}

    def remote(src, dst, send, recv, to):
        return pltpu.make_async_remote_copy(
            src_ref=src, dst_ref=dst, send_sem=send, recv_sem=recv,
            device_id=at(to), device_id_type=MESH,
        )

    def columns_of(chip_index):
        return pl.ds(pl.multiple_of(chip_index * wide, wide), wide)

    shifts = [s for s in range(stops) if s != reach]
    targets = [lax.rem(me + (s - reach) * group + mom_size, mom_size) for s in shifts]

    own_copy = pltpu.make_async_copy(green, gathered.at[member], small_sems.at[0])
    own_copy.start()
    small = [
        pltpu.make_async_copy(modes_hbm, modes, small_sems.at[1]),
        pltpu.make_async_copy(weights_hbm, weights, small_sems.at[2]),
    ]
    for copy in small:
        copy.start()
    loads = []
    for b in range(bank_size):
        for part in range(2):
            load = pltpu.make_async_copy(
                couplings.at[b, part],
                bank.at[b, :, pl.ds(part * order, order)],
                bank_sem.at[b, part],
            )
            load.start()
            loads.append(load)

    barrier = pltpu.get_barrier_semaphore()
    neighbours = [base + lax.rem(member + d, group) for d in range(1, group)] + targets
    for neighbour in neighbours:
        pl.semaphore_signal(barrier, inc=1, device_id=at(neighbour), device_id_type=MESH)
    pl.semaphore_wait(barrier, len(neighbours))

    chip_copies = {}
    for e in range(chips):
        for d in range(1, chips):
            other = lax.rem(chip + d, chips)
            columns = columns_of(lax.rem(other + e, chips))
            copy = remote(
                green.at[:, :, columns], gathered.at[member, :, :, columns],
                chip_sems.at[e, d, 0], chip_sems.at[e, d, 1], base + other * 2 + core,
            )
            copy.start()
            chip_copies[e, d] = copy
    pair_copy = remote(green, gathered.at[member], pair_sems.at[0], pair_sems.at[1], mate)
    pair_copy.start()

    relays = []

    def collect(e):
        latest = []
        for d in range(1, chips):
            source = lax.rem(chip + chips - d, chips) * 2 + core
            columns = columns_of(lax.rem(chip + e, chips))
            chip_copies[e, d].wait_recv()
            relay = remote(
                gathered.at[source, :, :, columns], gathered.at[source, :, :, columns],
                relay_sems.at[e, d, 0], relay_sems.at[e, d, 1], mate,
            )
            relay.start()
            latest.append(relay)
        relays.extend(latest)
        return latest

    def first_products(chip_index):
        for half in range(2):
            j = chip_index * 2 + half
            columns = pl.ds(pl.multiple_of(j * tile, tile), tile)
            beyond = pl.ds(pl.multiple_of(order + j * tile, tile), tile)
            mirror = [
                jnp.concatenate(
                    [gathered[i, part, :, columns].T for i in range(group)], axis=1
                ).astype(f32)
                for part in range(2)
            ]
            spec_real = (-(gathered[j, 1].astype(f32) + mirror[1])).astype(bf16)
            spec_imag = (gathered[j, 0].astype(f32) - mirror[0]).astype(bf16)
            rows_stack[half, pl.ds(0, tile), pl.ds(0, order)] = spec_real
            rows_stack[half, pl.ds(0, tile), pl.ds(order, order)] = spec_imag
            rows_stack[half, pl.ds(tile, tile), pl.ds(0, order)] = -spec_imag
            rows_stack[half, pl.ds(tile, tile), pl.ds(order, order)] = spec_real
            both = lax.dot_general(
                left[...], rows_stack[half], NT, preferred_element_type=f32
            ).astype(bf16)
            for b in range(bank_size):
                block = both[b * tile : (b + 1) * tile]
                real, imag = block[:, :tile], block[:, tile:]
                product[b, pl.ds(0, tile), columns] = real
                product[b, pl.ds(0, tile), beyond] = imag
                product[b, pl.ds(tile, tile), columns] = imag
                product[b, pl.ds(tile, tile), beyond] = -real

    for copy in small:
        copy.wait()
    scale = [
        [
            sum(
                jnp.where(modes[s, m] == b, weights[s, m], jnp.float32(0.0))
                for m in range(mode_count)
            )
            for b in range(bank_size)
        ]
        for s in range(stops)
    ]
    for load in loads:
        load.wait()
    for b in range(bank_size):
        left[pl.ds(b * tile, tile), :] = bank[b, pl.ds(pl.multiple_of(member * tile, tile), tile), :]

    own_copy.wait()
    latest = collect(0)
    pair_copy.wait_recv()
    for relay in latest:
        relay.wait_recv()
    first_products(chip)
    waits = []
    for e in range(1, chips):
        waits += collect(e)
    for relay in waits:
        relay.wait_recv()
    for e in range(1, chips):
        first_products(lax.rem(chip + e, chips))

    def chosen(d):
        other = lax.rem(chip + d, chips)
        later = jnp.where(other > chip, 1, 0)
        return other, core * later + (1 - core) * (1 - later)

    def second_products(d):
        other, pick = chosen(d)
        rows = columns_of(other)
        terms = [
            lax.dot_general(product[b], bank[b, rows, :], NT, preferred_element_type=f32)
            for b in range(bank_size)
        ]
        for index, s in enumerate(shifts):
            combined = sum(scale[s][b] * terms[b] for b in range(bank_size)).astype(bf16)
            outgoing[index, d, 0] = combined[:, :tile]
            outgoing[index, d, 1] = combined[:, tile:]
            term_copy(index, d).start()
            if d == 0:
                @pl.when(core == 0)
                def _():
                    mate_copy(index).start()
        combined = sum(scale[reach][b] * terms[b] for b in range(bank_size))
        own[d, 0] = combined[:, :tile]
        own[d, 1] = combined[:, tile:]

    def term_copy(index, d):
        pick = core if d == 0 else chosen(d)[1]
        return remote(
            outgoing.at[index, d, pick], incoming.at[index, d],
            term_sems.at[index, d, 0], term_sems.at[index, d, 1], targets[index],
        )

    def mate_copy(index):
        return remote(
            outgoing.at[index, 0, 1], mate_incoming.at[index],
            mate_term_sems.at[index, 0], mate_term_sems.at[index, 1], targets[index],
        )

    def mirror_copy(d):
        to = mate if d == 0 else base + chosen(d)[0] * 2 + chosen(d)[1]
        return remote(
            mirror_out.at[d], mirror_in.at[d], mirror_sems.at[d, 0], mirror_sems.at[d, 1], to
        )

    def received(d):
        total = None
        for index in range(len(shifts)):
            term_copy(index, d).wait_recv()
            piece = incoming[index, d].astype(f32)
            total = piece if total is None else total + piece
        return total

    def put(j, value):
        columns = pl.ds(pl.multiple_of(j * tile, tile), tile)
        out[0, :, columns] = value[:tile]
        out[1, :, columns] = value[tile:]

    def mirrored(d):
        block = mirror_in[d]
        return jnp.concatenate([block[:tile].T.astype(f32), -block[tile:].T.astype(f32)], axis=0)

    for d in list(range(1, chips)) + [0]:
        second_products(d)
    for d in range(1, chips):
        other, pick = chosen(d)
        total = received(d)
        mirror_out[d] = total.astype(bf16)
        mirror_copy(d).start()
        put(other * 2 + pick, own[d, pick] + total)

    @pl.when(core == 0)
    def _():
        total = None
        for index in range(len(shifts)):
            mate_copy(index).wait_recv()
            piece = mate_incoming[index].astype(f32)
            total = piece if total is None else total + piece
        mirror_out[0] = total.astype(bf16)
        mirror_copy(0).start()
        put(chip * 2 + 1, own[0, 1] + total)

    for d in range(1, chips):
        source = lax.rem(chip + chips - d, chips)
        slot = chips - d
        same = jnp.where(source < chip, 1, 0)
        which = core * same + (1 - core) * (1 - same)
        mirror_copy(d).wait_recv()
        put(source * 2 + which, own[slot, which] + mirrored(d))

    put(member, own[0, core] + received(0))

    @pl.when(core == 1)
    def _():
        mirror_copy(0).wait_recv()
        put(chip * 2, own[0, 0] + mirrored(0))

    for copy in chip_copies.values():
        copy.wait_send()
    pair_copy.wait_send()
    for relay in relays:
        relay.wait_send()
    for index in range(len(shifts)):
        for d in range(chips):
            term_copy(index, d).wait_send()
    for d in range(1, chips):
        mirror_copy(d).wait_send()

    @pl.when(core == 0)
    def _():
        for index in range(len(shifts)):
            mate_copy(index).wait_send()
        mirror_copy(0).wait_send()


def body(green_function, couplings, phonon_modes, weights):
    _, tile, order = green_function.shape
    group = order // tile
    chips = group // 2
    bank_size = couplings.shape[0]
    stops, mode_count = phonon_modes.shape
    dims = (lax.axis_size("mom"), group, tile, order, bank_size, stops, mode_count)
    bf16, f32 = jnp.bfloat16, jnp.float32
    flops = 8 * bank_size * tile * order * order * 2
    dma = pltpu.SemaphoreType.DMA
    return pl.pallas_call(
        functools.partial(kernel, dims),
        out_shape=jax.ShapeDtypeStruct((2, tile, order), f32),
        in_specs=[pl.BlockSpec(memory_space=pltpu.HBM)] * 4,
        out_specs=pl.BlockSpec(memory_space=pltpu.VMEM),
        scratch_shapes=[
            pltpu.SMEM((stops, mode_count), jnp.int32),
            pltpu.SMEM((stops, mode_count), f32),
            pltpu.VMEM((group, 2, tile, order), bf16),
            pltpu.VMEM((bank_size, order, 2 * order), bf16),
            pltpu.VMEM((bank_size * tile, 2 * order), bf16),
            pltpu.VMEM((2, 2 * tile, 2 * order), bf16),
            pltpu.VMEM((bank_size, 2 * tile, 2 * order), bf16),
            pltpu.VMEM((chips, 2, 2 * tile, tile), f32),
            pltpu.VMEM((stops - 1, chips, 2, 2 * tile, tile), bf16),
            pltpu.VMEM((stops - 1, chips, 2 * tile, tile), bf16),
            pltpu.VMEM((stops - 1, 2 * tile, tile), bf16),
            pltpu.VMEM((chips, 2 * tile, tile), bf16),
            pltpu.VMEM((chips, 2 * tile, tile), bf16),
            dma((3,)),
            dma((bank_size, 2)),
            dma((2,)),
            dma((chips, chips, 2)),
            dma((chips, chips, 2)),
            dma((stops - 1, chips, 2)),
            dma((stops - 1, 2)),
            dma((chips, 2)),
        ],
        compiler_params=pltpu.CompilerParams(
            collective_id=0, has_side_effects=True, vmem_limit_bytes=63 * 2**20
        ),
        cost_estimate=pl.CostEstimate(flops=flops, bytes_accessed=10 * 2**20, transcendentals=0),
    )(green_function, couplings, phonon_modes, weights)


def solution(mesh):
    in_specs = (P(None, ("grp", "mom"), None), P(), P(), P())
    out_specs = P(None, ("grp", "mom"), None)
    return jax.shard_map(body, mesh=mesh, in_specs=in_specs, out_specs=out_specs, check_vma=False)
```

time: 34.6 us -> 30.8 us (0.89)
  Pallas kernels: 31.3 us -> 28.7 us
  local copies, waits for them, and re-layouts: 3.11 us -> 1.87 us
    pallas_call x1, Pallas kernels: 31.3 us -> 28.7 us  [body(): pl.pallas_call(functools.partial(kernel, dims), out_shape=jax.ShapeDtypeS...]
    unnamed x7 -> x1, local copies, waits for them, and re-layouts: 3.11 us -> 1.87 us
where the time goes in v2:
time: 30.8 us; the launch traced here: 30.6 us
  Pallas kernels  28.7 us (93%)
  local copies, waits for them, and re-layouts  1.87 us (6%)
    pallas_call x1, Pallas kernels, body(): pl.pallas_call(functools.partial(kernel, dims), out_shape=jax.ShapeDtypeS...  28.7 us
    unnamed x1, local copies, waits for them, and re-layouts  1.87 us

profile of v2, /device:TPU:0, one launch (start us, length us, event | category | flops | bytes accessed | tf_op | source)
XLA Modules:
  0.0 30.6 jit_solution(13209720704985857288)
XLA Ops:
  0.0 28.7 %shard_map.46 = f32[2,128,512]{2,1,0:T(8,128)} custom-call(bf16[2,128,512]{2,1,0:T(8,128)(2,1)} %green.1, bf16[8,2,512,512]{3,2,1,0:T(8,128)(2,1)} %couplings.1, s32[3,4]{1,0:T(4,128)} %modes_hbm.1, f32[3,4]{1,0:T(4,128)} %weights_hbm.1), custom_call_target="tpu_custom_call" | custom-call | flops 4294967296 | bytes 10485760 | tf_op jit(solution)/shard_map/pallas_call | solution.py:287
  28.7 1.9 %copy.6 = f32[2,128,512]{2,1,0:T(8,128)} copy(f32[2,128,512]{2,1,0:T(8,128)} %shard_map.46) | data formatting | bytes 1048576

commit v3 on v2

--- a/solution.py
+++ b/solution.py
@@ -13,8 +13,8 @@
 
 def kernel(
     dims, green, couplings, modes_hbm, weights_hbm, out,
-    modes, weights, gathered, bank, left, rows_stack, product,
-    own, outgoing, incoming, mate_incoming, mirror_out, mirror_in,
+    modes, weights, gathered, bank, left, mirrors, rows_stack, product,
+    own, outgoing, incoming, packed_out, packed_in, mate_incoming, mirror_out, mirror_in,
     small_sems, bank_sem, pair_sems, chip_sems, relay_sems, term_sems, mate_term_sems,
     mirror_sems,
 ):
@@ -101,19 +101,22 @@
         relays.extend(latest)
         return latest
 
+    def mirror_tiles(column_chip, row_chip):
+        for half in range(2):
+            columns = pl.ds(pl.multiple_of((column_chip * 2 + half) * tile, tile), tile)
+            for lane in range(2):
+                i = row_chip * 2 + lane
+                place = pl.ds(pl.multiple_of(i * tile, tile), tile)
+                for part in range(2):
+                    mirrors[half, part, :, place] = gathered[i, part, :, columns].T
+
     def first_products(chip_index):
         for half in range(2):
             j = chip_index * 2 + half
             columns = pl.ds(pl.multiple_of(j * tile, tile), tile)
             beyond = pl.ds(pl.multiple_of(order + j * tile, tile), tile)
-            mirror = [
-                jnp.concatenate(
-                    [gathered[i, part, :, columns].T for i in range(group)], axis=1
-                ).astype(f32)
-                for part in range(2)
-            ]
-            spec_real = (-(gathered[j, 1].astype(f32) + mirror[1])).astype(bf16)
-            spec_imag = (gathered[j, 0].astype(f32) - mirror[0]).astype(bf16)
+            spec_real = (-(gathered[j, 1].astype(f32) + mirrors[half, 1].astype(f32))).astype(bf16)
+            spec_imag = (gathered[j, 0].astype(f32) - mirrors[half, 0].astype(f32)).astype(bf16)
             rows_stack[half, pl.ds(0, tile), pl.ds(0, order)] = spec_real
             rows_stack[half, pl.ds(0, tile), pl.ds(order, order)] = spec_imag
             rows_stack[half, pl.ds(tile, tile), pl.ds(0, order)] = -spec_imag
@@ -147,23 +150,35 @@
         left[pl.ds(b * tile, tile), :] = bank[b, pl.ds(pl.multiple_of(member * tile, tile), tile), :]
 
     own_copy.wait()
+    pair_copy.wait_recv()
+    mirror_tiles(chip, chip)
     latest = collect(0)
-    pair_copy.wait_recv()
     for relay in latest:
         relay.wait_recv()
+    for e in range(1, chips):
+        mirror_tiles(chip, lax.rem(chip + e, chips))
     first_products(chip)
     waits = []
+    if chips == 2:
+        mirror_tiles(1 - chip, chip)
     for e in range(1, chips):
         waits += collect(e)
     for relay in waits:
         relay.wait_recv()
     for e in range(1, chips):
-        first_products(lax.rem(chip + e, chips))
+        column_chip = lax.rem(chip + e, chips)
+        for d in range(1 if chips == 2 else 0, chips):
+            mirror_tiles(column_chip, lax.rem(chip + d, chips))
+        first_products(column_chip)
 
     def chosen(d):
         other = lax.rem(chip + d, chips)
         later = jnp.where(other > chip, 1, 0)
         return other, core * later + (1 - core) * (1 - later)
+
+    upper = lax.broadcasted_iota(jnp.int32, (tile, tile), 0) <= lax.broadcasted_iota(
+        jnp.int32, (tile, tile), 1
+    )
 
     def second_products(d):
         other, pick = chosen(d)
@@ -173,9 +188,12 @@
             for b in range(bank_size)
         ]
         for index, s in enumerate(shifts):
-            combined = sum(scale[s][b] * terms[b] for b in range(bank_size)).astype(bf16)
-            outgoing[index, d, 0] = combined[:, :tile]
-            outgoing[index, d, 1] = combined[:, tile:]
+            combined = sum(scale[s][b] * terms[b] for b in range(bank_size))
+            outgoing[index, d, 0] = combined[:, :tile].astype(bf16)
+            outgoing[index, d, 1] = combined[:, tile:].astype(bf16)
+            if d == 0:
+                half = jnp.where(core == 0, combined[:, :tile], combined[:, tile:])
+                packed_out[index] = jnp.where(upper, half[:tile], half[tile:]).astype(bf16)
             term_copy(index, d).start()
             if d == 0:
                 @pl.when(core == 0)
@@ -186,9 +204,13 @@
         own[d, 1] = combined[:, tile:]
 
     def term_copy(index, d):
-        pick = core if d == 0 else chosen(d)[1]
+        if d == 0:
+            return remote(
+                packed_out.at[index], packed_in.at[index],
+                term_sems.at[index, d, 0], term_sems.at[index, d, 1], targets[index],
+            )
         return remote(
-            outgoing.at[index, d, pick], incoming.at[index, d],
+            outgoing.at[index, d, chosen(d)[1]], incoming.at[index, d],
             term_sems.at[index, d, 0], term_sems.at[index, d, 1], targets[index],
         )
 
@@ -208,7 +230,7 @@
         total = None
         for index in range(len(shifts)):
             term_copy(index, d).wait_recv()
-            piece = incoming[index, d].astype(f32)
+            piece = (packed_in[index] if d == 0 else incoming[index, d]).astype(f32)
             total = piece if total is None else total + piece
         return total
 
@@ -249,7 +271,19 @@
         mirror_copy(d).wait_recv()
         put(source * 2 + which, own[slot, which] + mirrored(d))
 
-    put(member, own[0, core] + received(0))
+    packed = received(0)
+    turned = packed.T
+    below = lax.broadcasted_iota(jnp.int32, (tile, tile), 0) - lax.broadcasted_iota(
+        jnp.int32, (tile, tile), 1
+    )
+    diagonal = jnp.concatenate(
+        [
+            jnp.where(below <= 0, packed, turned),
+            jnp.where(below > 0, packed, jnp.where(below < 0, -turned, 0.0)),
+        ],
+        axis=0,
+    )
+    put(member, own[0, core] + diagonal)
 
     @pl.when(core == 1)
     def _():
@@ -295,11 +329,14 @@
             pltpu.VMEM((group, 2, tile, order), bf16),
             pltpu.VMEM((bank_size, order, 2 * order), bf16),
             pltpu.VMEM((bank_size * tile, 2 * order), bf16),
+            pltpu.VMEM((2, 2, tile, order), bf16),
             pltpu.VMEM((2, 2 * tile, 2 * order), bf16),
             pltpu.VMEM((bank_size, 2 * tile, 2 * order), bf16),
             pltpu.VMEM((chips, 2, 2 * tile, tile), f32),
             pltpu.VMEM((stops - 1, chips, 2, 2 * tile, tile), bf16),
             pltpu.VMEM((stops - 1, chips, 2 * tile, tile), bf16),
+            pltpu.VMEM((stops - 1, tile, tile), bf16),
+            pltpu.VMEM((stops - 1, tile, tile), bf16),
             pltpu.VMEM((stops - 1, 2 * tile, tile), bf16),
             pltpu.VMEM((chips, 2 * tile, tile), bf16),
             pltpu.VMEM((chips, 2 * tile, tile), bf16),

time: 30.8 us -> 29.8 us (0.968); the launches traced: 30.6 us -> 29.2 us
  Pallas kernels: 28.7 us -> 27.3 us
    pallas_call x1, Pallas kernels: 28.7 us -> 27.3 us  [body(): pl.pallas_call(functools.partial(kernel, dims), out_shape=jax.ShapeDtypeS...]
where the time goes in v3:
time: 29.8 us; the launch traced here: 29.2 us
  Pallas kernels  27.3 us (92%)
  local copies, waits for them, and re-layouts  1.87 us (6%)
    pallas_call x1, Pallas kernels, body(): pl.pallas_call(functools.partial(kernel, dims), out_shape=jax.ShapeDtypeS...  27.3 us
    unnamed x1, local copies, waits for them, and re-layouts  1.87 us

profile of v3, /device:TPU:0, one launch (start us, length us, event | category | flops | bytes accessed | tf_op | source)
XLA Modules:
  0.0 29.2 jit_solution(7438712561047643486)
XLA Ops:
  0.0 27.3 %shard_map.46 = f32[2,128,512]{2,1,0:T(8,128)} custom-call(bf16[2,128,512]{2,1,0:T(8,128)(2,1)} %green.1, bf16[8,2,512,512]{3,2,1,0:T(8,128)(2,1)} %couplings.1, s32[3,4]{1,0:T(4,128)} %modes_hbm.1, f32[3,4]{1,0:T(4,128)} %weights_hbm.1), custom_call_target="tpu_custom_call" | custom-call | flops 4294967296 | bytes 10485760 | tf_op jit(solution)/shard_map/pallas_call | solution.py:321
  27.3 1.9 %copy.6 = f32[2,128,512]{2,1,0:T(8,128)} copy(f32[2,128,512]{2,1,0:T(8,128)} %shard_map.46) | data formatting | bytes 1048576
